TPU v7x, 512 devices: a whole 4x4x16 slice. The times are simulated.
512 devices in a mesh: section: 32 (over z, core), row: 16 (over y, x).
Axes of the slice: x: 4, y: 4, z: 16, core: 2. Of those that a mesh axis runs over, the one named last changes fastest.
Arguments:
- section_inputs: bfloat16 [32, 2048, 2048], P('section', 'row'), may hold values from -6 to 6
- fresh_group: bfloat16 [2048, 2048], P('row'), may hold values from -6 to 6
- resident_state: float32 [32, 8, 128, 128], P('section'), may hold values from -162.9174 to 162.9174
- qkv_weight: bfloat16 [32, 2048, 3072], P('section', 'row'), may hold values from -0.125 to 0.125
- out_weight: bfloat16 [32, 1024, 2048], P('section', 'row'), may hold values from -0.1875 to 0.1875
- input_gain: float32 [32, 2048], P('section'), may hold values from 0.1 to 1.9
- head_gain: float32 [32, 1024], P('section'), may hold values from 0.1 to 1.9
Outputs:
- section_outputs: bfloat16 [32, 2048, 2048], P('section', 'row')
- final_state: float32 [32, 8, 128, 128], P('section')
All inputs are finite; a program needn't handle non-finite values.
Results may differ from a plain program's by a relative error of at most 0.01.
Values may be sent and summed in bfloat16 or wider, within the bound.
A program may use at most 64 MiB of HBM per device.

v0:
```python
import jax
import jax.numpy as jnp
from jax import lax
from jax.sharding import PartitionSpec as P


def passed_along(value, axis, by):
    peers = lax.axis_size(axis)
    pairs = [(i, i + by) for i in range(peers) if 0 <= i + by < peers]
    return lax.ppermute(value, axis, pairs)


def layer(inputs, state, qkv_full, out_full, input_gain, head_gain):
    rows = inputs.shape[0]
    heads = state.shape[0]
    head_size = state.shape[1]
    width = heads * head_size
    wide = inputs.astype(jnp.float32)
    normed = (
        wide * lax.rsqrt(jnp.mean(wide * wide, axis=-1, keepdims=True) + 1e-05) * input_gain
    ).astype(jnp.bfloat16)
    projected = jnp.dot(normed, qkv_full, preferred_element_type=jnp.float32)
    queries = jax.nn.silu(projected[:, :width]).astype(jnp.bfloat16).reshape(rows, heads, head_size)
    key_rows = (
        jax.nn.silu(projected[:, width : 2 * width])
        .astype(jnp.bfloat16)
        .reshape(rows, heads, head_size)
    )
    value_rows = projected[:, 2 * width :].astype(jnp.bfloat16).reshape(rows, heads, head_size)
    own_state = jnp.einsum("jhd,jhe->hde", key_rows, value_rows, preferred_element_type=jnp.float32)
    every = lax.all_gather(own_state[None].astype(jnp.bfloat16), "row", axis=0, tiled=True).astype(
        jnp.float32
    )
    order = lax.iota(jnp.int32, every.shape[0])
    earlier = (order < lax.axis_index("row")).astype(jnp.float32)
    before = jnp.sum(every * earlier[:, None, None, None], axis=0)
    total = jnp.sum(every, axis=0)
    prefix = state + before
    carried = jnp.einsum("ihd,hde->ihe", queries.astype(jnp.float32), prefix)
    scores = jnp.einsum("ihd,jhd->hij", queries, key_rows, preferred_element_type=jnp.float32)
    causal = lax.broadcasted_iota(jnp.int32, (rows, rows), 0) >= lax.broadcasted_iota(
        jnp.int32, (rows, rows), 1
    )
    weights = jnp.where(causal[None], scores, 0.0).astype(jnp.bfloat16)
    local = jnp.einsum("hij,jhe->ihe", weights, value_rows, preferred_element_type=jnp.float32)
    attended = carried + local
    scaled = attended * lax.rsqrt(jnp.mean(attended * attended, axis=-1, keepdims=True) + 1e-06)
    head_out = (scaled.reshape(rows, width) * head_gain).astype(jnp.bfloat16)
    result = (wide + jnp.dot(head_out, out_full, preferred_element_type=jnp.float32)).astype(
        jnp.bfloat16
    )
    return (result, state + total)


def body(
    section_inputs, fresh_group, resident_state, qkv_weight, out_weight, input_gain, head_gain
):
    qkv_full, out_full = (
        lax.all_gather(qkv_weight[0], "row", axis=0, tiled=True),
        lax.all_gather(out_weight[0], "row", axis=0, tiled=True),
    )
    first_out, first_state = layer(
        section_inputs[0], resident_state[0], qkv_full, out_full, input_gain[0], head_gain[0]
    )
    arrived = passed_along(first_out, "section", 1)
    second_in = jnp.where(lax.axis_index("section") == 0, fresh_group, arrived)
    second_out, second_state = layer(
        second_in, first_state, qkv_full, out_full, input_gain[0], head_gain[0]
    )
    return (second_out[None], second_state[None])


def solution(mesh):
    in_specs = (
        P("section", "row", None),
        P("row", None),
        P("section", None, None, None),
        P("section", "row", None),
        P("section", "row", None),
        P("section", None),
        P("section", None),
    )
    out_specs = (P("section", "row", None), P("section", None, None, None))
    return jax.shard_map(body, mesh=mesh, in_specs=in_specs, out_specs=out_specs, check_vma=False)
```

profile of v0, /device:TPU:1, one launch (start us, length us, event | category | flops | bytes accessed | tf_op | source)
XLA Modules:
  0.0 372.2 jit_solution(13485516950461262047)
XLA Ops:
  7.2 0.7 all-gather.9.cloned.1.call-update
  7.9 1.2 fusion.32
  9.2 112.5 %all-gather.9.cloned.1.call-done = bf16[1,2048,3072]{2,1,0:T(8,128)(2,1)} async-done(((bf16[1,128,3072]{2,1,0:T(8,128)(2,1)}), bf16[1,2048,3072]{2,1,0:T(8,128)(2,1)}) %all-gather.9.cloned.1.call-update) | async-done | bytes 12582928 | tf_op jit(solution)/shard_map/all_gather | solution.py:59
  121.7 6.7 %fusion.2 = f32[128,3072]{1,0:T(8,128)S(1)} fusion(bf16[1,2048,3072]{2,1,0:T(8,128)(2,1)} %all-gather.9.cloned.1.call-done, bf16[1,128,2048]{2,1,0:T(8,128)(2,1)} %param.7, f32[2048]{0:T(1024)} %bitcast.105, f32[128]{0:T(128)S(1)} %add_rsqrt_fusion.3), kind=kOutput, calls=%fused_computation.2 | convolution fusion | flops 1611661312 | bytes 14688768 | tf_op jit(solution)/shard_map/dot_general | solution.py:22
  128.4 0.3 fusion.56
  129.1 1.0 convolution_convert_fusion.1
  130.1 0.7 all-gather.13.cloned.1.call-update
  130.9 66.0 %all-gather.11.cloned.1.call-done = bf16[128,128,128]{2,1,0:T(8,128)(2,1)} async-done(((bf16[8,128,128]{2,1,0:T(8,128)(2,1)}), bf16[128,128,128]{2,1,0:T(8,128)(2,1)}) %all-gather.11.cloned.1.call-update) | async-done | bytes 4194320 | tf_op jit(solution)/shard_map/all_gather | solution.py:31
  196.9 3.6 convert_reduce_fusion.1
  200.4 0.3 fusion.40
  200.8 0.5 multiply_reduce_fusion.1
  201.6 65.0 %all-gather.13.cloned.1.call-done = bf16[1,1024,2048]{2,1,0:T(8,128)(2,1)} async-done(((bf16[1,64,2048]{2,1,0:T(8,128)(2,1)}), bf16[1,1024,2048]{2,1,0:T(8,128)(2,1)}) %all-gather.13.cloned.1.call-update) | async-done | bytes 4194320 | tf_op jit(solution)/shard_map/all_gather | solution.py:60
  266.5 2.9 fusion.19
  269.5 3.7 %collective-permute-start = (bf16[128,2048]{1,0:T(8,128)(2,1)S(1)}, bf16[128,2048]{1,0:T(8,128)(2,1)S(1)}, u32[]{:S(2)}, u32[]{:S(2)}) collective-permute-start(bf16[128,2048]{1,0:T(8,128)(2,1)S(1)} %fusion.19), channel_id=1, source_target_pairs={{0,16},{16,32},{32,48},{48,64},{64,80},{80,96},{96,112},{112,128},... | collective-permute-start | bytes 1572872 | tf_op jit(solution)/shard_map/ppermute | solution.py:10
  273.2 6.1 %collective-permute-done = bf16[128,2048]{1,0:T(8,128)(2,1)S(1)} collective-permute-done((bf16[128,2048]{1,0:T(8,128)(2,1)S(1)}, bf16[128,2048]{1,0:T(8,128)(2,1)S(1)}, u32[]{:S(2)}, u32[]{:S(2)}) %collective-permute-start) | collective-permute-done | bytes 524320 | tf_op jit(solution)/shard_map/ppermute | solution.py:10
  279.6 6.5 %fusion = f32[128,3072]{1,0:T(8,128)S(1)} fusion(bf16[1,2048,3072]{2,1,0:T(8,128)(2,1)} %all-gather.9.cloned.1.call-done, bf16[128,2048]{1,0:T(8,128)(2,1)S(1)} %get-tuple-element.7, f32[128]{0:T(128)S(1)} %add_rsqrt_fusion.2, f32[2048]{0:T(1024)S(1)} %bitcast.106), kind=kOutput, calls=%fused_computation | convolution fusion | flops 1611661312 | bytes 14688768 | tf_op jit(solution)/shard_map/dot_general | solution.py:22
  286.1 0.3 fusion.57
  286.8 1.0 convolution_convert_fusion
  287.9 68.6 %all-gather.15.cloned.1.call-done = bf16[128,128,128]{2,1,0:T(8,128)(2,1)} async-done(((bf16[8,128,128]{2,1,0:T(8,128)(2,1)}), bf16[128,128,128]{2,1,0:T(8,128)(2,1)}) %all-gather.15.cloned.1.call-update) | async-done | bytes 4194320 | tf_op jit(solution)/shard_map/all_gather | solution.py:31
  356.5 3.5 convert_reduce_fusion
  360.0 0.9 bitcast_add_fusion
  360.9 0.3 fusion.42
  361.2 0.5 multiply_reduce_fusion
  362.0 3.7 %fusion.22 = bf16[1,128,2048]{2,1,0:T(8,128)(2,1)} fusion(bf16[128,1024]{0,1:T(8,128)(2,1)S(1)} %fusion.37, bf16[1,1024,2048]{2,1,0:T(8,128)(2,1)} %all-gather.13.cloned.1.call-done, bf16[128,2048]{1,0:T(8,128)(2,1)S(1)} %get-tuple-element.7), kind=kOutput, calls=%fused_computation.18 | convolution fusion | flops 537657344 | bytes 5505024 | tf_op jit(solution)/shard_map/dot_general | solution.py:49
  (33 shorter events, 1.8 us)
Async XLA Ops:
  7.2 114.5 %all-gather.9.cloned.1.call-start = ((), (), s32[]{:S(2)}) async-start(), calls=%async_computation | async-start | bytes 13369344 | tf_op jit(solution)/shard_map/all_gather | solution.py:59
  7.9 189.0 %all-gather.11.cloned.1.call-start = ((), (), s32[]{:S(2)}) async-start(), calls=%async_computation.1 | async-start | bytes 4456448 | tf_op jit(solution)/shard_map/all_gather | solution.py:31
  128.6 71.8 %copy-start.1 = (f32[1,8,128,128]{3,2,1,0:T(8,128)S(1)}, f32[1,8,128,128]{3,2,1,0:T(8,128)}, u32[]{:S(2)}) copy-start(f32[1,8,128,128]{3,2,1,0:T(8,128)} %param.9) | copy-start | bytes 1572868
  130.1 136.5 %all-gather.13.cloned.1.call-start = ((), (), s32[]{:S(2)}) async-start(), calls=%async_computation.2 | async-start | bytes 4456448 | tf_op jit(solution)/shard_map/all_gather | solution.py:60
  130.8 225.7 %all-gather.15.cloned.1.call-start = ((), (), s32[]{:S(2)}) async-start(), calls=%async_computation.3 | async-start | bytes 4456448 | tf_op jit(solution)/shard_map/all_gather | solution.py:31
  196.9 4.5 %copy-start.4 = (f32[1,1024]{1,0:T(1,128)S(1)}, f32[1,1024]{1,0:T(1,128)}, u32[]{:S(2)}) copy-start(f32[1,1024]{1,0:T(1,128)} %param.13) | copy-start | bytes 12292
  196.9 69.7 %copy-start = (bf16[1,128,2048]{2,1,0:T(8,128)(2,1)S(1)}, bf16[1,128,2048]{2,1,0:T(8,128)(2,1)}, u32[]{:S(2)}) copy-start(bf16[1,128,2048]{2,1,0:T(8,128)(2,1)} %param.7) | copy-start | bytes 1572868
  201.2 78.1 %copy-start.2 = (bf16[128,2048]{1,0:T(8,128)(2,1)S(1)}, bf16[128,2048]{1,0:T(8,128)(2,1)}, u32[]{:S(2)}) copy-start(bf16[128,2048]{1,0:T(8,128)(2,1)} %param.8) | copy-start | bytes 1572868
  201.3 78.3 %copy-start.3 = (f32[1,2048]{1,0:T(1,128)S(1)}, f32[1,2048]{1,0:T(1,128)}, u32[]{:S(2)}) copy-start(f32[1,2048]{1,0:T(1,128)} %param.12) | copy-start | bytes 24580
  269.5 9.8 %collective-permute-start = (bf16[128,2048]{1,0:T(8,128)(2,1)S(1)}, bf16[128,2048]{1,0:T(8,128)(2,1)S(1)}, u32[]{:S(2)}, u32[]{:S(2)}) collective-permute-start(bf16[128,2048]{1,0:T(8,128)(2,1)S(1)} %fusion.19), channel_id=1, source_target_pairs={{0,16},{16,32},{32,48},{48,64},{64,80},{80,96},{96,112},{112,128},... | collective-permute-start | bytes 1572872 | tf_op jit(solution)/shard_map/ppermute | solution.py:10
Sparse Core Ops, SparseCore 0:
  11.0 110.6 all-gather.8
  130.2 66.6 all-gather.10
  199.9 66.6 all-gather.12
  288.0 68.4 all-gather.14
where the time goes:
time: 373 us; the launch traced here: 372 us
  waiting for transfers between devices  320 us (86%)
  matrix products  23.4 us (6%)
  between operations  14 us (4%)
  other arithmetic  10.6 us (3%)
  starting transfers between devices  3.89 us (1%)
    all_gather x2, waiting for transfers between devices, layer(): lax.all_gather(own_state[None].astype(jnp.bfloat16), 'row', axis=0, tiled...  135 us
    all_gather x1, waiting for transfers between devices, body(): lax.all_gather(qkv_weight[0], 'row', axis=0, tiled=True)  112 us
    all_gather x1, waiting for transfers between devices, body(): lax.all_gather(out_weight[0], 'row', axis=0, tiled=True)  65 us
    dot_general x2, matrix products, layer(): projected = jnp.dot(normed, qkv_full, preferred_element_type=jnp.float32)  13.2 us
  transfers between devices with their start and end apart: 5, of which 5 were waited for; matrix products, arithmetic and copies ran while one was open for 2% of the time, Pallas kernels for 0%

commit v1 on v0

--- a/solution.py
+++ b/solution.py
@@ -57,7 +57,9 @@
 ):
     qkv_full, out_full = (
         lax.all_gather(qkv_weight[0], "row", axis=0, tiled=True),
-        lax.all_gather(out_weight[0], "row", axis=0, tiled=True),
+        jnp.concatenate(
+            lax.all_to_all(jnp.stack([out_weight[0]] * lax.axis_size("row")), "row", 0, 0), axis=0
+        ),
     )
     first_out, first_state = layer(
         section_inputs[0], resident_state[0], qkv_full, out_full, input_gain[0], head_gain[0]

time: 373 us -> 338 us (0.906)
  waiting for transfers between devices: 320 us -> 277 us
  starting transfers between devices: 3.89 us -> 9.07 us
    all_gather x1 -> x0, waiting for transfers between devices: 65 us -> none  [body(): lax.all_gather(out_weight[0], 'row', axis=0, tiled=True)]
    all_gather x2, waiting for transfers between devices: 135 us -> 158 us  [layer(): lax.all_gather(own_state[None].astype(jnp.bfloat16), 'row', axis=0, tiled...]
    all_to_all x0 -> x1, starting transfers between devices: none -> 5.03 us  [body(): lax.all_to_all(jnp.stack([out_weight[0]] * lax.axis_size('row')), 'row',...]
  transfers between devices with their start and end apart: 5 -> 5, of which waited for: 5 -> 4; matrix products, arithmetic and copies ran while one was open for 2% -> 2% of each run, Pallas kernels for 0% -> 0%
where the time goes in v1:
time: 338 us; the launch traced here: 337 us
  waiting for transfers between devices  277 us (82%)
  matrix products  23.4 us (7%)
  between operations  14 us (4%)
  other arithmetic  10.5 us (3%)
  starting transfers between devices  9.07 us (3%)
    all_gather x2, waiting for transfers between devices, layer(): lax.all_gather(own_state[None].astype(jnp.bfloat16), 'row', axis=0, tiled...  158 us
    all_gather x1, waiting for transfers between devices, body(): lax.all_gather(qkv_weight[0], 'row', axis=0, tiled=True)  112 us
    dot_general x2, matrix products, layer(): projected = jnp.dot(normed, qkv_full, preferred_element_type=jnp.float32)  13.2 us
    reduce_sum x2, other arithmetic, layer(): total = jnp.sum(every, axis=0)  7.09 us
  transfers between devices with their start and end apart: 5, of which 4 were waited for; matrix products, arithmetic and copies ran while one was open for 2% of the time, Pallas kernels for 0%

profile of v1, /device:TPU:1, one launch (start us, length us, event | category | flops | bytes accessed | tf_op | source)
XLA Modules:
  0.0 337.4 jit_solution(17369476133870625532)
XLA Ops:
  7.2 0.7 all-gather.7.cloned.1.call-update
  7.9 1.2 fusion.16
  9.2 112.5 %all-gather.7.cloned.1.call-done = bf16[1,2048,3072]{2,1,0:T(8,128)(2,1)} async-done(((bf16[1,128,3072]{2,1,0:T(8,128)(2,1)}), bf16[1,2048,3072]{2,1,0:T(8,128)(2,1)}) %all-gather.7.cloned.1.call-update) | async-done | bytes 12582928 | tf_op jit(solution)/shard_map/all_gather | solution.py:59
  121.7 6.7 %fusion.2 = f32[128,3072]{1,0:T(8,128)S(1)} fusion(bf16[1,2048,3072]{2,1,0:T(8,128)(2,1)} %all-gather.7.cloned.1.call-done, bf16[1,128,2048]{2,1,0:T(8,128)(2,1)} %param.7, f32[2048]{0:T(1024)} %bitcast.90, f32[128]{0:T(128)S(1)} %add_rsqrt_fusion.3), kind=kOutput, calls=%fused_computation.2 | convolution fusion | flops 1611661312 | bytes 14688768 | tf_op jit(solution)/shard_map/dot_general | solution.py:22
  128.4 0.3 fusion.38
  129.0 1.0 convolution_convert_fusion.1
  130.1 2.5 stack.3
  132.6 5.0 %all-to-all-start = ((bf16[16,64,2048]{2,1,0:T(8,128)(2,1)}), bf16[16,64,2048]{2,1,0:T(8,128)(2,1)}, u32[]{:S(2)}, u32[]{:S(2)}) async-start(bf16[16,64,2048]{2,1,0:T(8,128)(2,1)} %stack.3), calls=%async_computation | async-start | bytes 8388608 | tf_op jit(solution)/shard_map/all_to_all | solution.py:61
  137.7 89.4 %all-gather.9.cloned.1.call-done = bf16[128,128,128]{2,1,0:T(8,128)(2,1)} async-done(((bf16[8,128,128]{2,1,0:T(8,128)(2,1)}), bf16[128,128,128]{2,1,0:T(8,128)(2,1)}) %all-gather.9.cloned.1.call-update) | async-done | bytes 4194320 | tf_op jit(solution)/shard_map/all_gather | solution.py:31
  227.1 3.6 %convert_reduce_fusion.1 = (f32[8,128,128]{2,1,0:T(8,128)S(1)}, f32[8,128,128]{2,1,0:T(8,128)S(1)}) fusion(bf16[16,8,128,128]{3,2,1,0:T(8,128)(2,1)} %bitcast.78, f32[16]{0:T(128)S(1)} %compare_convert_fusion), kind=kLoop, calls=%fused_computation.6 | loop fusion | flops 8126464 | bytes 5242944 | tf_op jit(solution)/shard_map/reduce_sum | solution.py:37
  230.7 0.3 fusion.22
  231.0 0.5 multiply_reduce_fusion.1
  231.8 2.9 fusion.6
  234.7 3.9 %collective-permute-start = (bf16[128,2048]{1,0:T(8,128)(2,1)S(1)}, bf16[128,2048]{1,0:T(8,128)(2,1)S(1)}, u32[]{:S(2)}, u32[]{:S(2)}) collective-permute-start(bf16[128,2048]{1,0:T(8,128)(2,1)S(1)} %fusion.6), channel_id=1, source_target_pairs={{0,16},{16,32},{32,48},{48,64},{64,80},{80,96},{96,112},{112,128},... | collective-permute-start | bytes 1572872 | tf_op jit(solution)/shard_map/ppermute | solution.py:10
  238.6 5.9 %collective-permute-done = bf16[128,2048]{1,0:T(8,128)(2,1)S(1)} collective-permute-done((bf16[128,2048]{1,0:T(8,128)(2,1)S(1)}, bf16[128,2048]{1,0:T(8,128)(2,1)S(1)}, u32[]{:S(2)}, u32[]{:S(2)}) %collective-permute-start) | collective-permute-done | bytes 524320 | tf_op jit(solution)/shard_map/ppermute | solution.py:10
  244.8 6.5 %fusion = f32[128,3072]{1,0:T(8,128)S(1)} fusion(bf16[1,2048,3072]{2,1,0:T(8,128)(2,1)} %all-gather.7.cloned.1.call-done, bf16[128,2048]{1,0:T(8,128)(2,1)S(1)} %get-tuple-element.7, f32[128]{0:T(128)S(1)} %add_rsqrt_fusion.2, f32[2048]{0:T(1024)S(1)} %bitcast.91), kind=kOutput, calls=%fused_computation | convolution fusion | flops 1611661312 | bytes 14688768 | tf_op jit(solution)/shard_map/dot_general | solution.py:22
  251.4 0.3 fusion.39
  252.0 1.0 convolution_convert_fusion
  253.1 68.6 %all-gather.11.cloned.1.call-done = bf16[128,128,128]{2,1,0:T(8,128)(2,1)} async-done(((bf16[8,128,128]{2,1,0:T(8,128)(2,1)}), bf16[128,128,128]{2,1,0:T(8,128)(2,1)}) %all-gather.11.cloned.1.call-update) | async-done | bytes 4194320 | tf_op jit(solution)/shard_map/all_gather | solution.py:31
  321.7 3.5 %convert_reduce_fusion = (f32[8,128,128]{2,1,0:T(8,128)S(1)}, f32[8,128,128]{2,1,0:T(8,128)S(1)}) fusion(bf16[16,8,128,128]{3,2,1,0:T(8,128)(2,1)} %bitcast.79, f32[16]{0:T(128)S(1)} %compare_convert_fusion), kind=kLoop, calls=%fused_computation.4 | loop fusion | flops 8126464 | bytes 5242944 | tf_op jit(solution)/shard_map/reduce_sum | solution.py:37
  325.2 0.9 bitcast_add_fusion
  326.1 0.3 fusion.24
  326.5 0.5 multiply_reduce_fusion
  327.1 3.7 %fusion.8 = bf16[1,128,2048]{2,1,0:T(8,128)(2,1)} fusion(bf16[128,1024]{0,1:T(8,128)(2,1)S(1)} %bitcast.89, bf16[1024,2048]{1,0:T(8,128)(2,1)} %bitcast.11, bf16[128,2048]{1,0:T(8,128)(2,1)S(1)} %get-tuple-element.7), kind=kOutput, calls=%fused_computation.14 | convolution fusion | flops 537657344 | bytes 5505024 | tf_op jit(solution)/shard_map/dot_general | solution.py:49
  (33 shorter events, 1.7 us)
Async XLA Ops:
  7.2 114.5 %all-gather.7.cloned.1.call-start = ((), (), s32[]{:S(2)}) async-start(), calls=%async_computation.1 | async-start | bytes 13369344 | tf_op jit(solution)/shard_map/all_gather | solution.py:59
  7.9 219.2 %all-gather.9.cloned.1.call-start = ((), (), s32[]{:S(2)}) async-start(), calls=%async_computation.2 | async-start | bytes 4456448 | tf_op jit(solution)/shard_map/all_gather | solution.py:31
  128.4 1.7 copy-start.4
  132.6 99.2 %all-to-all-start = ((bf16[16,64,2048]{2,1,0:T(8,128)(2,1)}), bf16[16,64,2048]{2,1,0:T(8,128)(2,1)}, u32[]{:S(2)}, u32[]{:S(2)}) async-start(bf16[16,64,2048]{2,1,0:T(8,128)(2,1)} %stack.3), calls=%async_computation | async-start | bytes 8388608 | tf_op jit(solution)/shard_map/all_to_all | solution.py:61
  137.6 93.1 %copy-start.1 = (f32[1,8,128,128]{3,2,1,0:T(8,128)S(1)}, f32[1,8,128,128]{3,2,1,0:T(8,128)}, u32[]{:S(2)}) copy-start(f32[1,8,128,128]{3,2,1,0:T(8,128)} %param.9) | copy-start | bytes 1572868
  137.6 184.1 %all-gather.11.cloned.1.call-start = ((), (), s32[]{:S(2)}) async-start(), calls=%async_computation.3 | async-start | bytes 4456448 | tf_op jit(solution)/shard_map/all_gather | solution.py:31
  227.1 4.4 %copy-start.5 = (f32[1,1024]{1,0:T(1,128)S(1)}, f32[1,1024]{1,0:T(1,128)}, u32[]{:S(2)}) copy-start(f32[1,1024]{1,0:T(1,128)} %param.13) | copy-start | bytes 12292
  227.1 4.7 %copy-start = (bf16[1,128,2048]{2,1,0:T(8,128)(2,1)S(1)}, bf16[1,128,2048]{2,1,0:T(8,128)(2,1)}, u32[]{:S(2)}) copy-start(bf16[1,128,2048]{2,1,0:T(8,128)(2,1)} %param.7) | copy-start | bytes 1572868
  231.5 13.1 %copy-start.2 = (bf16[128,2048]{1,0:T(8,128)(2,1)S(1)}, bf16[128,2048]{1,0:T(8,128)(2,1)}, u32[]{:S(2)}) copy-start(bf16[128,2048]{1,0:T(8,128)(2,1)} %param.8) | copy-start | bytes 1572868
  231.5 13.4 %copy-start.3 = (f32[1,2048]{1,0:T(1,128)S(1)}, f32[1,2048]{1,0:T(1,128)}, u32[]{:S(2)}) copy-start(f32[1,2048]{1,0:T(1,128)} %param.12) | copy-start | bytes 24580
  234.7 9.9 %collective-permute-start = (bf16[128,2048]{1,0:T(8,128)(2,1)S(1)}, bf16[128,2048]{1,0:T(8,128)(2,1)S(1)}, u32[]{:S(2)}, u32[]{:S(2)}) collective-permute-start(bf16[128,2048]{1,0:T(8,128)(2,1)S(1)} %fusion.6), channel_id=1, source_target_pairs={{0,16},{16,32},{32,48},{48,64},{64,80},{80,96},{96,112},{112,128},... | collective-permute-start | bytes 1572872 | tf_op jit(solution)/shard_map/ppermute | solution.py:10
Sparse Core Ops, SparseCore 0:
  11.0 110.6 all-gather.6
  130.2 96.8 all-gather.8
  253.2 68.4 all-gather.10
